TPU v7x, 32 devices: a whole 2x2x4 slice. The times are simulated.
32 devices in a mesh: groups: 2 (over y), adapter: 8 (over z, x), tensor: 2 (over core).
Axes of the slice: x: 2, y: 2, z: 4, core: 2. Of those that a mesh axis runs over, the one named last changes fastest.
Arguments:
- hidden_state_rows: bfloat16 [2048, 8192], P(('groups', 'adapter'), 'tensor'), parts along dimension 0, may hold values from -6 to 6
- value_weight: bfloat16 [8192, 512], P('tensor'), may hold values from -0.0625 to 0.0625
- adapter_down_weight: bfloat16 [16, 8192, 64], P(('groups', 'adapter'), 'tensor'), parts along dimension 0, may hold values from -0.0625 to 0.0625
- adapter_up_weight: bfloat16 [16, 64, 512], P(('groups', 'adapter'), None, 'tensor'), parts along dimension 0, may hold values from -0.75 to 0.75
- request_adapter_index: int32 [2048], P(('groups', 'adapter')), parts along dimension 0, may hold values from 0 to 7, as said below
Outputs:
- value_out: bfloat16 [2048, 512], P(('groups', 'adapter'), 'tensor'), parts along dimension 0
There are 2 independent parts, one for each index of `groups`. A program takes and returns all parts, laid end to end along the dimension named above; an argument that names none is the same for every part. Nothing has to cross between parts.
Inputs may be any that keep to these rules, and one draw needn't show every extreme that they name: `request_adapter_index`: within the rows of one device (aligned blocks of 128 rows) no adapter is named more than 17 times; one adapter, the same for every device, is named exactly 17 times in every block.
All inputs are finite; a program needn't handle non-finite values.
Results may differ from a plain program's by a relative error of at most 0.001.
Values may be sent and summed in bfloat16 or wider, within the bound.
A program may use at most 64 MiB of HBM per device.

v0:
```python
import jax
import jax.numpy as jnp
from jax import lax
from jax.sharding import PartitionSpec as P

highest_precision = lax.Precision.HIGHEST


def adapter_delta_rows(incoming_rows, down_matrix, up_matrix):
    flat_rows = incoming_rows.reshape(-1, incoming_rows.shape[-1])
    reduced_rows = jnp.dot(flat_rows, down_matrix, preferred_element_type=jnp.float32)
    reduced_rows = lax.psum(reduced_rows, "tensor")
    widened_rows = jnp.dot(
        reduced_rows, up_matrix, precision=highest_precision, preferred_element_type=jnp.float32
    )
    widened_rows = widened_rows.reshape(
        incoming_rows.shape[0], incoming_rows.shape[1], up_matrix.shape[1]
    )
    return lax.all_to_all(widened_rows, "adapter", split_axis=0, concat_axis=0, tiled=True)


def body(
    hidden_state_rows, value_weight, adapter_down_weight, adapter_up_weight, request_adapter_index
):
    holders = lax.axis_size("adapter")
    rows_here = hidden_state_rows.shape[0]
    slots_per_pair = 2 + (rows_here - 1) // holders
    holder_ids = lax.broadcasted_iota(jnp.int32, (rows_here, holders), 1)
    onehot = (request_adapter_index[:, None] == holder_ids).astype(jnp.int32)
    pair_ranks = jnp.sum(onehot * (jnp.cumsum(onehot, axis=0) - 1), axis=1)
    slot_index = request_adapter_index * slots_per_pair + pair_ranks
    down_matrix = adapter_down_weight[0]
    up_matrix = adapter_up_weight[0].astype(jnp.float32)
    slot_ids = lax.broadcasted_iota(jnp.int32, (holders * slots_per_pair, rows_here), 0)
    placing = (slot_ids == slot_index[None, :]).astype(hidden_state_rows.dtype)
    send_rows = jnp.dot(placing, hidden_state_rows, preferred_element_type=jnp.float32).astype(
        hidden_state_rows.dtype
    )
    send_rows = send_rows.reshape(holders, slots_per_pair, hidden_state_rows.shape[1])
    value_result = adapter_delta_rows(
        lax.all_to_all(send_rows, "adapter", split_axis=0, concat_axis=0, tiled=True),
        down_matrix,
        up_matrix,
    )
    delta_rows = jnp.take(value_result.reshape(holders * slots_per_pair, -1), slot_index, axis=0)
    base_terms = jnp.dot(hidden_state_rows, value_weight, preferred_element_type=jnp.float32)
    own_columns = lax.psum_scatter(base_terms, "tensor", scatter_dimension=1, tiled=True)
    summed = own_columns + delta_rows
    return summed.astype(jnp.bfloat16)


def solution(mesh):
    return jax.shard_map(
        body,
        mesh=mesh,
        in_specs=(
            P(("groups", "adapter"), "tensor"),
            P("tensor", None),
            P(("groups", "adapter"), "tensor", None),
            P(("groups", "adapter"), None, "tensor"),
            P(("groups", "adapter")),
        ),
        out_specs=P(("groups", "adapter"), "tensor"),
        check_vma=False,
    )
```

profile of v0, /device:TPU:0, one launch (start us, length us, event | category | flops | bytes accessed | tf_op | source)
XLA Modules:
  0.0 84.3 jit_solution(3923802128029020583)
XLA Ops:
  6.5 0.0 copy-start
  6.5 0.8 fusion.2
  7.4 0.2 reduce_window_sum.11
  7.5 0.8 select_reduce_fusion
  8.4 0.7 compare_and_fusion
  9.0 0.0 copy-done
  9.0 0.4 convolution_convert_fusion
  9.5 1.6 %reshape.18 = bf16[8,17,4096]{2,1,0:T(8,128)(2,1)} reshape(bf16[136,4096]{1,0:T(8,128)(2,1)S(1)} %convolution_convert_fusion) | data formatting | bytes 2228224 | tf_op jit(solution)/shard_map/reshape | solution.py:39
  11.0 7.3 %all-to-all-start = ((bf16[8,17,4096]{2,1,0:T(8,128)(2,1)}), bf16[8,17,4096]{2,1,0:T(8,128)(2,1)S(1)}, u32[]{:S(2)}, u32[]{:S(2)}) async-start(bf16[8,17,4096]{2,1,0:T(8,128)(2,1)} %reshape.18), calls=%async_computation.1 | async-start | bytes 3145728 | tf_op jit(solution)/shard_map/all_to_all | solution.py:41
  18.3 0.0 reduce-scatter.2.cloned.1.call-start
  18.3 3.6 %fusion.6 = f32[128,512]{1,0:T(8,128)} fusion(bf16[128,4096]{1,0:T(8,128)(2,1)S(1)} %copy-done, bf16[4096,512]{1,0:T(8,128)(2,1)} %param.6), kind=kOutput, calls=%fused_computation.16 | convolution fusion | flops 536870912 | bytes 5505024 | tf_op jit(solution)/shard_map/dot_general | solution.py:46
  22.0 0.0 copy-start.1
  22.0 0.0 reduce-scatter.2.cloned.1.call-update
  22.0 33.3 %all-to-all-done = bf16[8,17,4096]{2,1,0:T(8,128)(2,1)S(1)} async-done(((bf16[8,17,4096]{2,1,0:T(8,128)(2,1)}), bf16[8,17,4096]{2,1,0:T(8,128)(2,1)S(1)}, u32[]{:S(2)}, u32[]{:S(2)}) %all-to-all-start) | async-done | bytes 1114144 | tf_op jit(solution)/shard_map/all_to_all | solution.py:41
  55.3 1.4 %reshape.19 = bf16[136,4096]{1,0:T(8,128)(2,1)} reshape(bf16[8,17,4096]{2,1,0:T(8,128)(2,1)S(1)} %all-to-all-done) | data formatting | bytes 2228224 | tf_op jit(solution)/shard_map/reshape | solution.py:10
  56.7 0.0 copy-done.1
  56.7 0.0 copy-start.2
  56.7 1.7 %fusion = f32[136,64]{1,0:T(8,128)S(1)} fusion(bf16[136,4096]{1,0:T(8,128)(2,1)} %reshape.19, bf16[1,4096,64]{1,2,0:T(8,128)(2,1)S(1)} %copy-done.1), kind=kOutput, calls=%fused_computation.2 | convolution fusion | flops 71303168 | bytes 1673216 | tf_op jit(solution)/shard_map/dot_general | solution.py:11
  58.4 3.6 %psum.7 = f32[8,17,64]{2,1,0:T(8,128)S(1)} all-reduce(f32[8,17,64]{2,1,0:T(8,128)S(1)} %dot_general.17), channel_id=1, replica_groups=mesh['groups'=2,'adapter'=8,'tensor'=2] {'tensor'}, use_global_device_ids=true, to_apply=%region_3.4 | all-reduce | flops 8704 | bytes 69632 | tf_op jit(solution)/shard_map/psum | solution.py:12
  62.0 0.0 copy-done.2
  62.0 0.9 %fusion.4 = f32[8,17,256]{2,1,0:T(8,128)} fusion(f32[8,17,64]{2,1,0:T(8,128)S(1)} %psum.7, bf16[1,64,256]{2,1,0:T(8,128)(2,1)S(1)} %copy-done.2), kind=kOutput, calls=%fused_computation.10 | convolution fusion | flops 26738688 | bytes 206848 | tf_op jit(solution)/shard_map/dot_general | solution.py:13
  62.9 3.6 %all-to-all-start.1 = ((f32[8,17,256]{2,1,0:T(8,128)}), f32[8,17,256]{2,1,0:T(8,128)S(1)}, u32[]{:S(2)}, u32[]{:S(2)}) async-start(f32[8,17,256]{2,1,0:T(8,128)} %fusion.4), calls=%async_computation.2 | async-start | bytes 393216 | tf_op jit(solution)/shard_map/all_to_all | solution.py:19
  66.6 8.4 %all-to-all-done.1 = f32[8,17,256]{2,1,0:T(8,128)S(1)} async-done(((f32[8,17,256]{2,1,0:T(8,128)}), f32[8,17,256]{2,1,0:T(8,128)S(1)}, u32[]{:S(2)}, u32[]{:S(2)}) %all-to-all-start.1) | async-done | bytes 139296 | tf_op jit(solution)/shard_map/all_to_all | solution.py:19
  75.1 0.8 gather_fusion
  75.8 0.0 reduce-scatter.2.cloned.1.call-done
  75.8 1.6 %add_convert_fusion = bf16[128,256]{1,0:T(8,128)(2,1)} fusion(f32[128,256]{1,0:T(8,128)} %reduce-scatter.2.cloned.1.call-done, f32[128,256]{1,0:T(8,128)S(1)} %gather_fusion, pred[128]{0:T(512)(128)(4,1)S(1)} %get-tuple-element.5), kind=kLoop, calls=%fused_computation.4 | loop fusion | flops 98304 | bytes 327808 | tf_op jit(solution)/shard_map/convert_element_type | solution.py:49
  (4 shorter events, 0.0 us)
Async XLA Ops:
  6.5 2.5 %copy-start = (bf16[128,4096]{1,0:T(8,128)(2,1)S(1)}, bf16[128,4096]{1,0:T(8,128)(2,1)}, u32[]{:S(2)}) copy-start(bf16[128,4096]{1,0:T(8,128)(2,1)} %param.5) | copy-start | bytes 3145732
  11.0 44.3 %all-to-all-start = ((bf16[8,17,4096]{2,1,0:T(8,128)(2,1)}), bf16[8,17,4096]{2,1,0:T(8,128)(2,1)S(1)}, u32[]{:S(2)}, u32[]{:S(2)}) async-start(bf16[8,17,4096]{2,1,0:T(8,128)(2,1)} %reshape.18), calls=%async_computation.1 | async-start | bytes 3145728 | tf_op jit(solution)/shard_map/all_to_all | solution.py:41
  18.3 57.5 %reduce-scatter.2.cloned.1.call-start = ((), (), s32[]{:S(2)}) async-start(), calls=%async_computation.3 | async-start | bytes 393216 | tf_op jit(solution)/shard_map/reduce_scatter | solution.py:47
  22.0 34.8 %copy-start.1 = (bf16[1,4096,64]{1,2,0:T(8,128)(2,1)S(1)}, bf16[1,4096,64]{1,2,0:T(8,128)(2,1)}, u32[]{:S(2)}) copy-start(bf16[1,4096,64]{1,2,0:T(8,128)(2,1)} %param.7) | copy-start | bytes 1572868
  56.7 5.3 %copy-start.2 = (bf16[1,64,256]{2,1,0:T(8,128)(2,1)S(1)}, bf16[1,64,256]{2,1,0:T(8,128)(2,1)}, u32[]{:S(2)}) copy-start(bf16[1,64,256]{2,1,0:T(8,128)(2,1)} %param.8) | copy-start | bytes 98308
  62.9 12.1 %all-to-all-start.1 = ((f32[8,17,256]{2,1,0:T(8,128)}), f32[8,17,256]{2,1,0:T(8,128)S(1)}, u32[]{:S(2)}, u32[]{:S(2)}) async-start(f32[8,17,256]{2,1,0:T(8,128)} %fusion.4), calls=%async_computation.2 | async-start | bytes 393216 | tf_op jit(solution)/shard_map/all_to_all | solution.py:19
Sparse Core Ops, SparseCore 0:
  22.1 9.0 reduce-scatter.1
where the time goes:
time: 84.7 us; the launch traced here: 84.3 us
  waiting for transfers between devices  41.8 us (49%)
  between operations  13.5 us (16%)
  starting transfers between devices  10.9 us (13%)
  matrix products  6.65 us (8%)
  other arithmetic  4.13 us (5%)
  local copies, waits for them, and re-layouts  3.76 us (4%)
  blocking collectives  3.59 us (4%)
    all_to_all x1, waiting for transfers between devices, body(): lax.all_to_all(send_rows, 'adapter', split_axis=0, concat_axis=0, tiled=T...  33.3 us
    all_to_all x1, waiting for transfers between devices, adapter_delta_rows(): lax.all_to_all(widened_rows, 'adapter', split_axis=0, concat_axis=0, tile...  8.43 us
    all_to_all x1, starting transfers between devices, body(): lax.all_to_all(send_rows, 'adapter', split_axis=0, concat_axis=0, tiled=T...  7.26 us
    all_to_all x1, starting transfers between devices, adapter_delta_rows(): lax.all_to_all(widened_rows, 'adapter', split_axis=0, concat_axis=0, tile...  3.63 us
    dot_general x1, matrix products, body(): jnp.dot(hidden_state_rows, value_weight, preferred_element_type=jnp.float32)  3.61 us
    psum x1, blocking collectives, adapter_delta_rows(): reduced_rows = lax.psum(reduced_rows, 'tensor')  3.59 us
    dot_general x1, matrix products, adapter_delta_rows(): jnp.dot(flat_rows, down_matrix, preferred_element_type=jnp.float32)  1.7 us
  transfers between devices with their start and end apart: 3, of which 2 were waited for; matrix products, arithmetic and copies ran while one was open for 10% of the time, Pallas kernels for 0%

commit v1 on v0

--- a/solution.py
+++ b/solution.py
@@ -1,9 +1,259 @@
+import functools
+
 import jax
 import jax.numpy as jnp
 from jax import lax
+from jax.experimental import pallas as pl
+from jax.experimental.pallas import tpu as pltpu
 from jax.sharding import PartitionSpec as P
 
 highest_precision = lax.Precision.HIGHEST
+BLOCK = 16
+f32 = jnp.float32
+bf16 = jnp.bfloat16
+
+
+def dot(a, b):
+    return jnp.dot(a, b, preferred_element_type=f32)
+
+
+def three_parts(x):
+    high = x.astype(bf16)
+    rest = x - high.astype(f32)
+    middle = rest.astype(bf16)
+    low = (rest - middle.astype(f32)).astype(bf16)
+    return high, middle, low
+
+
+def adapter_kernel(
+    n, groups, index_ref, hidden_hbm, value_hbm, down_hbm, up_hbm, out_ref,
+    hidden, value, down, up, rows_out, rows_in, spill_out, spill_in,
+    part_out, part_in, delta_out, delta_in, spill_delta_out, spill_delta_in,
+    base_own, base_out, base_in,
+    load_sem, rows_sem, spill_sem, part_sem, delta_sem, spill_delta_sem, base_sem,
+):
+    me = lax.axis_index("adapter")
+    core = lax.axis_index("tensor")
+    rows, depth = hidden.shape
+    width = value.shape[1]
+    half = width // 2
+    rank = up.shape[0]
+    chunks = depth // 128
+
+    loads = [
+        pltpu.make_async_copy(src, dst, load_sem.at[i])
+        for i, (src, dst) in enumerate(
+            ((hidden_hbm, hidden), (down_hbm, down), (up_hbm, up), (value_hbm, value))
+        )
+    ]
+    for load in loads:
+        load.start()
+
+    barrier = pltpu.get_barrier_semaphore()
+    for k in range(1, n):
+        pl.semaphore_signal(barrier, inc=1, device_id={"adapter": me ^ k})
+    pl.semaphore_signal(barrier, inc=1, device_id={"tensor": 1 - core})
+
+    def push(src, dst, sems, k, target):
+        copy = pltpu.make_async_remote_copy(
+            src_ref=src, dst_ref=dst, send_sem=sems.at[0, k], recv_sem=sems.at[1, k],
+            device_id=target,
+        )
+        copy.start()
+        return copy
+
+    block_of = index_ref[...] ^ me
+    member = (lax.broadcasted_iota(jnp.int32, (n, rows), 0) == block_of).astype(f32)
+    earlier = (
+        lax.broadcasted_iota(jnp.int32, (rows, rows), 0)
+        < lax.broadcasted_iota(jnp.int32, (rows, rows), 1)
+    ).astype(bf16)
+    place = jnp.sum(member * dot(member.astype(bf16), earlier), axis=0, keepdims=True)
+    place = place.astype(jnp.int32)
+    main_slot = jnp.where(place < BLOCK, block_of * BLOCK + place, -1)
+    spill_block = jnp.where(place == BLOCK, block_of, -1)
+    main_pick = lax.broadcasted_iota(jnp.int32, (n * BLOCK, rows), 0) == main_slot
+    spill_pick = lax.broadcasted_iota(jnp.int32, (n, rows), 0) == spill_block
+    pick = jnp.concatenate([main_pick.astype(f32), spill_pick.astype(f32)], axis=0).astype(bf16)
+    eighth = lax.broadcasted_iota(jnp.int32, (n * 8, rows), 0)
+    back = jnp.concatenate(
+        [
+            main_pick.astype(f32),
+            (eighth == spill_block * 8).astype(f32),
+            (eighth == spill_block * 8 + 1).astype(f32),
+        ],
+        axis=0,
+    )
+    back = jnp.transpose(back).astype(bf16)
+    turn_row = lax.broadcasted_iota(jnp.int32, (n * chunks, n * chunks), 0)
+    turn_column = lax.broadcasted_iota(jnp.int32, (n * chunks, n * chunks), 1)
+
+    loads[0].wait()
+    picked = dot(pick, hidden[...])
+    rows_out[...] = picked[: n * BLOCK].astype(bf16).reshape(n, BLOCK, depth)
+    turn = (turn_row % chunks * n + turn_row // chunks == turn_column).astype(bf16)
+    spilled = jnp.concatenate(
+        [picked[n * BLOCK :, c * 128 : (c + 1) * 128] for c in range(chunks)], axis=0
+    ).astype(bf16)
+    spill_out[...] = dot(turn, spilled).astype(bf16).reshape(n, chunks, 128)
+
+    pl.semaphore_wait(barrier, n)
+    spill_copies = {}
+    row_copies = {}
+    for k in range(1, n):
+        spill_copies[k] = push(
+            spill_out.at[k], spill_in.at[k], spill_sem, k, {"adapter": me ^ k}
+        )
+    for k in [k for group in groups for k in group if k > 0]:
+        row_copies[k] = push(rows_out.at[k], rows_in.at[k], rows_sem, k, {"adapter": me ^ k})
+
+    loads[3].wait()
+    base = dot(hidden[...], value[...])
+    first, second = base[:, :half], base[:, half:]
+    base_own[...] = jnp.where(core == 0, first, second)
+    base_out[...] = jnp.where(core == 0, second, first)
+    base_copy = push(base_out, base_in, base_sem, 0, {"tensor": 1 - core})
+
+    loads[1].wait()
+    loads[2].wait()
+    rows_in[0] = rows_out[0]
+    spill_in[0] = spill_out[0]
+
+    def shrink_part(block):
+        part = dot(block, down[...])
+        return jnp.concatenate([part, jnp.zeros((part.shape[0], 128 - rank), f32)], axis=1)
+
+    def widen(reduced):
+        count = reduced.shape[0]
+        stacked = jnp.concatenate([x.astype(f32) for x in three_parts(reduced)], axis=0)
+        wide = dot(stacked.astype(bf16), up[...])
+        return wide[:count] + wide[count : 2 * count] + wide[2 * count :]
+
+    part_copies = []
+    delta_copies = []
+    spill_delta_copies = []
+
+    def exchange(start, count, slot):
+        region = pl.ds(start, count)
+        copy = push(part_out.at[region], part_in.at[region], part_sem, slot, {"tensor": 1 - core})
+        part_copies.append(copy)
+        copy.wait_recv()
+        return (part_out[region] + part_in[region])[:, :rank]
+
+    for g, group in enumerate(groups):
+        for k in group:
+            if k > 0:
+                row_copies[k].wait_recv()
+        begin, count = group[0] * BLOCK, len(group) * BLOCK
+        block = rows_in[group[0] : group[0] + len(group)].reshape(count, depth)
+        part_out[pl.ds(begin, count)] = shrink_part(block)
+        deltas = widen(exchange(begin, count, g)).reshape(len(group), BLOCK, half)
+        for i, k in enumerate(group):
+            if k == 0:
+                delta_in[0] = deltas[i]
+            else:
+                delta_out[k] = deltas[i]
+                delta_copies.append(
+                    push(delta_out.at[k], delta_in.at[k], delta_sem, k, {"adapter": me ^ k})
+                )
+        if g == 0:
+            for k in range(1, n):
+                spill_copies[k].wait_recv()
+            turn_back = (turn_row % n * chunks + turn_row // n == turn_column).astype(bf16)
+            turned = dot(turn_back, spill_in[...].reshape(n * chunks, 128))
+            spilled = jnp.concatenate(
+                [turned[c * n : (c + 1) * n] for c in range(chunks)], axis=1
+            ).astype(bf16)
+            part_out[pl.ds(n * BLOCK, n)] = shrink_part(spilled)
+            wide = widen(exchange(n * BLOCK, n, len(groups)))
+            spill_delta_out[...] = jnp.zeros_like(spill_delta_out)
+            for k in range(n):
+                spill_delta_out[k, 0:1, :] = wide[k : k + 1, :128]
+                spill_delta_out[k, 1:2, :] = wide[k : k + 1, 128:]
+            spill_delta_in[0] = spill_delta_out[0]
+            for k in range(1, n):
+                spill_delta_copies.append(
+                    push(
+                        spill_delta_out.at[k], spill_delta_in.at[k], spill_delta_sem, k,
+                        {"adapter": me ^ k},
+                    )
+                )
+
+    base_copy.wait_recv()
+    total = base_own[...] + base_in[...]
+    for copy in spill_delta_copies:
+        copy.wait_recv()
+    spill_deltas = spill_delta_in[...].reshape(n * 8, 128)
+    low = sum(dot(back[:, n * BLOCK : n * BLOCK + n * 8], x) for x in three_parts(spill_deltas))
+    high = sum(dot(back[:, n * BLOCK + n * 8 :], x) for x in three_parts(spill_deltas))
+    total = total + jnp.concatenate([low, high], axis=1)
+    for copy in delta_copies:
+        copy.wait_recv()
+    deltas = delta_in[...].reshape(n * BLOCK, half)
+    total = total + sum(dot(back[:, : n * BLOCK], x) for x in three_parts(deltas))
+    out_ref[...] = total.astype(out_ref.dtype)
+
+    for copy in [*spill_copies.values(), *row_copies.values(), *part_copies, *delta_copies,
+                 *spill_delta_copies, base_copy]:
+        copy.wait_send()
+
+
+def fused_body(
+    hidden_state_rows, value_weight, adapter_down_weight, adapter_up_weight, request_adapter_index
+):
+    n = lax.axis_size("adapter")
+    rows, depth = hidden_state_rows.shape
+    width = value_weight.shape[1]
+    half = width // 2
+    rank = adapter_down_weight.shape[2]
+    chunks = depth // 128
+    groups = GROUPS
+    dma = pltpu.SemaphoreType.DMA
+    return pl.pallas_call(
+        functools.partial(adapter_kernel, n, groups),
+        out_shape=jax.ShapeDtypeStruct((rows, half), bf16),
+        in_specs=[pl.BlockSpec(memory_space=pltpu.VMEM)]
+        + [pl.BlockSpec(memory_space=pl.ANY)] * 4,
+        out_specs=pl.BlockSpec(memory_space=pltpu.VMEM),
+        scratch_shapes=[
+            pltpu.VMEM((rows, depth), bf16),
+            pltpu.VMEM((depth, width), bf16),
+            pltpu.VMEM((depth, rank), bf16),
+            pltpu.VMEM((rank, half), bf16),
+            pltpu.VMEM((n, BLOCK, depth), bf16),
+            pltpu.VMEM((n, BLOCK, depth), bf16),
+            pltpu.VMEM((n, chunks, 128), bf16),
+            pltpu.VMEM((n, chunks, 128), bf16),
+            pltpu.VMEM((n * BLOCK + n, 128), f32),
+            pltpu.VMEM((n * BLOCK + n, 128), f32),
+            pltpu.VMEM((n, BLOCK, half), f32),
+            pltpu.VMEM((n, BLOCK, half), f32),
+            pltpu.VMEM((n, 8, 128), f32),
+            pltpu.VMEM((n, 8, 128), f32),
+            pltpu.VMEM((rows, half), f32),
+            pltpu.VMEM((rows, half), f32),
+            pltpu.VMEM((rows, half), f32),
+            dma((4,)),
+            dma((2, n)),
+            dma((2, n)),
+            dma((2, n + 1)),
+            dma((2, n)),
+            dma((2, n)),
+            dma((2, 1)),
+        ],
+        compiler_params=pltpu.CompilerParams(
+            collective_id=0, has_side_effects=True, vmem_limit_bytes=40 * 1024 * 1024
+        ),
+    )(
+        request_adapter_index.reshape(1, rows),
+        hidden_state_rows,
+        value_weight,
+        adapter_down_weight.reshape(depth, rank),
+        adapter_up_weight.reshape(rank, half),
+    )
+
+
+GROUPS = ((0, 1), (2, 3), (4, 5), (6, 7))
 
 
 def adapter_delta_rows(incoming_rows, down_matrix, up_matrix):
@@ -19,7 +269,7 @@
     return lax.all_to_all(widened_rows, "adapter", split_axis=0, concat_axis=0, tiled=True)
 
 
-def body(
+def general_body(
     hidden_state_rows, value_weight, adapter_down_weight, adapter_up_weight, request_adapter_index
 ):
     holders = lax.axis_size("adapter")
@@ -49,6 +299,13 @@
     return summed.astype(jnp.bfloat16)
 
 
+def body(*arrays):
+    n = lax.axis_size("adapter")
+    if n == 8 and arrays[0].shape[0] == n * BLOCK:
+        return fused_body(*arrays)
+    return general_body(*arrays)
+
+
 def solution(mesh):
     return jax.shard_map(
         body,

time: 84.7 us -> 44.7 us (0.53)
  the two profiles are of different devices: /device:TPU:0 before, /device:TPU:9 now
where the time goes in v1:
time: 44.7 us; the launch traced here: 44.4 us
  Pallas kernels  37.4 us (84%)
  local copies, waits for them, and re-layouts  6.97 us (16%)
    pallas_call x1, Pallas kernels, fused_body(): pl.pallas_call(functools.partial(adapter_kernel, n, groups), out_shape=ja...  37.4 us
    unnamed x10, local copies, waits for them, and re-layouts  6.97 us

profile of v1, /device:TPU:9, one launch (start us, length us, event | category | flops | bytes accessed | tf_op | source)
XLA Modules:
  0.0 44.4 jit_solution(17583472349581827532)
XLA Ops:
  0.0 1.5 %copy.6 = bf16[1,4096,64]{2,1,0:T(8,128)(2,1)S(1)} copy(bf16[1,4096,64]{1,2,0:T(8,128)(2,1)} %param.7) | data formatting | bytes 1048576 | tf_op args[2]
  1.5 0.0 copy-start
  1.5 2.2 %copy-done = bf16[4096,512]{1,0:T(8,128)(2,1)S(1)} copy-done((bf16[4096,512]{1,0:T(8,128)(2,1)S(1)}, bf16[4096,512]{1,0:T(8,128)(2,1)}, u32[]{:S(2)}) %copy-start) | copy-done | bytes 4194328
  3.7 0.0 copy-start.1
  3.7 1.2 %copy-done.1 = bf16[128,4096]{1,0:T(8,128)(2,1)S(1)} copy-done((bf16[128,4096]{1,0:T(8,128)(2,1)S(1)}, bf16[128,4096]{1,0:T(8,128)(2,1)}, u32[]{:S(2)}) %copy-start.1) | copy-done | bytes 1048600
  4.9 0.0 copy-start.2
  4.9 0.8 %copy-done.2 = bf16[1,64,256]{2,1,0:T(8,128)(2,1)S(1)} copy-done((bf16[1,64,256]{2,1,0:T(8,128)(2,1)S(1)}, bf16[1,64,256]{2,1,0:T(8,128)(2,1)}, u32[]{:S(2)}) %copy-start.2) | copy-done | bytes 32792
  5.7 0.0 copy-start.3
  5.7 0.7 %copy-done.3 = s32[128]{0:T(128)S(1)} copy-done((s32[128]{0:T(128)S(1)}, s32[128]{0:T(128)}, u32[]{:S(2)}) %copy-start.3) | copy-done | bytes 536
  6.4 37.4 %shard_map.55 = bf16[128,256]{1,0:T(8,128)(2,1)S(1)} custom-call(s32[1,128]{1,0:T(1,128)S(1)} %bitcast.5, bf16[128,4096]{1,0:T(8,128)(2,1)S(1)} %copy-done.1, bf16[4096,512]{1,0:T(8,128)(2,1)S(1)} %copy-done, bf16[4096,64]{1,0:T(8,128)(2,1)S(1)} %bitcast.3, bf16[64,256]{1,0:T(8,128)(2,1)S(1)} %bitcast.4), custom_call_target="tpu_custom_call" | custom-call | tf_op jit(solution)/shard_map/pallas_call | solution.py:212
  43.7 0.6 %copy.8 = bf16[128,256]{1,0:T(8,128)(2,1)} copy(bf16[128,256]{1,0:T(8,128)(2,1)S(1)} %shard_map.55) | data formatting | bytes 131072
Async XLA Ops:
  1.5 2.2 %copy-start = (bf16[4096,512]{1,0:T(8,128)(2,1)S(1)}, bf16[4096,512]{1,0:T(8,128)(2,1)}, u32[]{:S(2)}) copy-start(bf16[4096,512]{1,0:T(8,128)(2,1)} %value_hbm.1) | copy-start | bytes 12582916
  3.7 1.2 %copy-start.1 = (bf16[128,4096]{1,0:T(8,128)(2,1)S(1)}, bf16[128,4096]{1,0:T(8,128)(2,1)}, u32[]{:S(2)}) copy-start(bf16[128,4096]{1,0:T(8,128)(2,1)} %hidden_hbm.1) | copy-start | bytes 3145732
  4.9 0.8 %copy-start.2 = (bf16[1,64,256]{2,1,0:T(8,128)(2,1)S(1)}, bf16[1,64,256]{2,1,0:T(8,128)(2,1)}, u32[]{:S(2)}) copy-start(bf16[1,64,256]{2,1,0:T(8,128)(2,1)} %param.8) | copy-start | bytes 98308
  5.7 0.7 %copy-start.3 = (s32[128]{0:T(128)S(1)}, s32[128]{0:T(128)}, u32[]{:S(2)}) copy-start(s32[128]{0:T(128)} %param.9) | copy-start | bytes 1540

commit v2 on v1

--- a/solution.py
+++ b/solution.py
@@ -26,8 +26,8 @@
 
 
 def adapter_kernel(
-    n, groups, index_ref, hidden_hbm, value_hbm, down_hbm, up_hbm, out_ref,
-    hidden, value, down, up, rows_out, rows_in, spill_out, spill_in,
+    n, groups, index_hbm, hidden_hbm, value_hbm, down_hbm, up_hbm, out_ref,
+    index, hidden, value, down, up, rows_out, rows_in, spill_out, spill_in,
     part_out, part_in, delta_out, delta_in, spill_delta_out, spill_delta_in,
     base_own, base_out, base_in,
     load_sem, rows_sem, spill_sem, part_sem, delta_sem, spill_delta_sem, base_sem,
@@ -43,7 +43,10 @@
     loads = [
         pltpu.make_async_copy(src, dst, load_sem.at[i])
         for i, (src, dst) in enumerate(
-            ((hidden_hbm, hidden), (down_hbm, down), (up_hbm, up), (value_hbm, value))
+            (
+                (index_hbm, index), (hidden_hbm, hidden), (down_hbm, down), (up_hbm, up),
+                (value_hbm, value),
+            )
         )
     ]
     for load in loads:
@@ -62,7 +65,8 @@
         copy.start()
         return copy
 
-    block_of = index_ref[...] ^ me
+    loads[0].wait()
+    block_of = index[...] ^ me
     member = (lax.broadcasted_iota(jnp.int32, (n, rows), 0) == block_of).astype(f32)
     earlier = (
         lax.broadcasted_iota(jnp.int32, (rows, rows), 0)
@@ -88,7 +92,7 @@
     turn_row = lax.broadcasted_iota(jnp.int32, (n * chunks, n * chunks), 0)
     turn_column = lax.broadcasted_iota(jnp.int32, (n * chunks, n * chunks), 1)
 
-    loads[0].wait()
+    loads[1].wait()
     picked = dot(pick, hidden[...])
     rows_out[...] = picked[: n * BLOCK].astype(bf16).reshape(n, BLOCK, depth)
     turn = (turn_row % chunks * n + turn_row // chunks == turn_column).astype(bf16)
@@ -107,20 +111,22 @@
     for k in [k for group in groups for k in group if k > 0]:
         row_copies[k] = push(rows_out.at[k], rows_in.at[k], rows_sem, k, {"adapter": me ^ k})
 
-    loads[3].wait()
+    loads[4].wait()
     base = dot(hidden[...], value[...])
     first, second = base[:, :half], base[:, half:]
     base_own[...] = jnp.where(core == 0, first, second)
     base_out[...] = jnp.where(core == 0, second, first)
     base_copy = push(base_out, base_in, base_sem, 0, {"tensor": 1 - core})
 
-    loads[1].wait()
     loads[2].wait()
+    loads[3].wait()
     rows_in[0] = rows_out[0]
     spill_in[0] = spill_out[0]
 
     def shrink_part(block):
-        part = dot(block, down[...])
+        part = lax.dot_general(
+            block, down[...], (((1,), (1,)), ((), ())), preferred_element_type=f32
+        )
         return jnp.concatenate([part, jnp.zeros((part.shape[0], 128 - rank), f32)], axis=1)
 
     def widen(reduced):
@@ -212,13 +218,13 @@
     return pl.pallas_call(
         functools.partial(adapter_kernel, n, groups),
         out_shape=jax.ShapeDtypeStruct((rows, half), bf16),
-        in_specs=[pl.BlockSpec(memory_space=pltpu.VMEM)]
-        + [pl.BlockSpec(memory_space=pl.ANY)] * 4,
+        in_specs=[pl.BlockSpec(memory_space=pl.ANY)] * 5,
         out_specs=pl.BlockSpec(memory_space=pltpu.VMEM),
         scratch_shapes=[
+            pltpu.VMEM((1, rows), jnp.int32),
             pltpu.VMEM((rows, depth), bf16),
             pltpu.VMEM((depth, width), bf16),
-            pltpu.VMEM((depth, rank), bf16),
+            pltpu.VMEM((rank, depth), bf16),
             pltpu.VMEM((rank, half), bf16),
             pltpu.VMEM((n, BLOCK, depth), bf16),
             pltpu.VMEM((n, BLOCK, depth), bf16),
@@ -233,7 +239,7 @@
             pltpu.VMEM((rows, half), f32),
             pltpu.VMEM((rows, half), f32),
             pltpu.VMEM((rows, half), f32),
-            dma((4,)),
+            dma((5,)),
             dma((2, n)),
             dma((2, n)),
             dma((2, n + 1)),
@@ -242,13 +248,13 @@
             dma((2, 1)),
         ],
         compiler_params=pltpu.CompilerParams(
-            collective_id=0, has_side_effects=True, vmem_limit_bytes=40 * 1024 * 1024
+            collective_id=0, has_side_effects=True, vmem_limit_bytes=60 * 1024 * 1024
         ),
     )(
         request_adapter_index.reshape(1, rows),
         hidden_state_rows,
         value_weight,
-        adapter_down_weight.reshape(depth, rank),
+        jnp.swapaxes(adapter_down_weight.reshape(depth, rank), 0, 1),
         adapter_up_weight.reshape(rank, half),
     )
 

time: 44.7 us -> 39.3 us (0.88)
  local copies, waits for them, and re-layouts: 6.97 us -> 1.47 us
    unnamed x10 -> x1, local copies, waits for them, and re-layouts: 6.97 us -> 1.47 us
where the time goes in v2:
time: 39.3 us; the launch traced here: 39.1 us
  Pallas kernels  37.6 us (96%)
  local copies, waits for them, and re-layouts  1.47 us (4%)
    pallas_call x1, Pallas kernels, fused_body(): pl.pallas_call(functools.partial(adapter_kernel, n, groups), out_shape=ja...  37.6 us
    unnamed x1, local copies, waits for them, and re-layouts  1.47 us

profile of v2, /device:TPU:9, one launch (start us, length us, event | category | flops | bytes accessed | tf_op | source)
XLA Modules:
  0.0 39.1 jit_solution(8543398946987163853)
XLA Ops:
  0.0 37.6 %shard_map.55 = bf16[128,256]{1,0:T(8,128)(2,1)} custom-call(s32[1,128]{1,0:T(1,128)} %bitcast.7, bf16[128,4096]{1,0:T(8,128)(2,1)} %hidden_hbm.1, bf16[4096,512]{1,0:T(8,128)(2,1)} %value_hbm.1, bf16[64,4096]{1,0:T(8,128)(2,1)} %bitcast.5, bf16[64,256]{1,0:T(8,128)(2,1)} %bitcast.6), custom_call_target="tpu_custom_call" | custom-call | tf_op jit(solution)/shard_map/pallas_call | solution.py:218
  37.6 1.5 %copy.7 = bf16[128,256]{1,0:T(8,128)(2,1)} copy(bf16[128,256]{1,0:T(8,128)(2,1)} %shard_map.55) | data formatting | bytes 131072

commit v3 on v2

v3 whole, which is shorter than its diff:
```python
import functools

import jax
import jax.numpy as jnp
from jax import lax
from jax.experimental import pallas as pl
from jax.experimental.pallas import tpu as pltpu
from jax.sharding import PartitionSpec as P

highest_precision = lax.Precision.HIGHEST
BLOCK = 16
f32 = jnp.float32
bf16 = jnp.bfloat16


def dot(a, b):
    return jnp.dot(a, b, preferred_element_type=f32)


def three_parts(x):
    high = x.astype(bf16)
    rest = x - high.astype(f32)
    middle = rest.astype(bf16)
    low = (rest - middle.astype(f32)).astype(bf16)
    return high, middle, low


def adapter_kernel(
    n, groups, index_hbm, hidden_hbm, value_hbm, down_hbm, up_hbm, out_ref,
    index, hidden, value, down, up, rows_out, rows_in, part_out, part_in, delta_out, delta_in,
    base_own, base_out, base_in,
    load_sem, rows_sem, part_sem, delta_sem, base_sem,
):
    me = lax.axis_index("adapter")
    core = lax.axis_index("tensor")
    rows, depth = hidden.shape
    width = value.shape[1]
    half = width // 2
    rank = up.shape[0]
    chunks = depth // 128
    main = chunks * BLOCK
    each = len(groups[0])
    count = each * BLOCK

    loads = [
        pltpu.make_async_copy(src, dst, load_sem.at[i])
        for i, (src, dst) in enumerate(
            (
                (index_hbm, index), (hidden_hbm, hidden), (down_hbm, down), (up_hbm, up),
                (value_hbm, value),
            )
        )
    ]
    loads[0].start()
    loads[1].start()

    barrier = pltpu.get_barrier_semaphore()
    for k in range(1, n):
        pl.semaphore_signal(barrier, inc=1, device_id={"adapter": me ^ k})
    pl.semaphore_signal(barrier, inc=1, device_id={"tensor": 1 - core})

    sent = []

    def push(src, dst, sems, k, target):
        copy = pltpu.make_async_remote_copy(
            src_ref=src, dst_ref=dst, send_sem=sems.at[0, k], recv_sem=sems.at[1, k],
            device_id=target,
        )
        copy.start()
        sent.append(copy)
        return copy

    loads[0].wait()
    block_of = index[...] ^ me
    member = (lax.broadcasted_iota(jnp.int32, (n, rows), 0) == block_of).astype(f32)
    earlier = (
        lax.broadcasted_iota(jnp.int32, (rows, rows), 0)
        < lax.broadcasted_iota(jnp.int32, (rows, rows), 1)
    ).astype(bf16)
    place = jnp.sum(member * dot(member.astype(bf16), earlier), axis=0, keepdims=True)
    place = place.astype(jnp.int32)
    main_slot = jnp.where(place < BLOCK, block_of * BLOCK + place, -1)
    spill_block = jnp.where(place == BLOCK, block_of, -1)
    main_pick = lax.broadcasted_iota(jnp.int32, (n * BLOCK, rows), 0) == main_slot
    spill_pick = lax.broadcasted_iota(jnp.int32, (n, rows), 0) == spill_block
    pick = jnp.concatenate([main_pick.astype(f32), spill_pick.astype(f32)], axis=0).astype(bf16)
    turn_row = lax.broadcasted_iota(jnp.int32, (n * chunks, n * chunks), 0)
    turn_column = lax.broadcasted_iota(jnp.int32, (n * chunks, n * chunks), 1)
    turn = (turn_row % chunks * n + turn_row // chunks == turn_column).astype(bf16)

    loads[1].wait()
    for load in loads[2:]:
        load.start()
    picked = dot(pick, hidden[...])
    for c in range(chunks):
        rows_out[:, c * BLOCK : (c + 1) * BLOCK, :] = (
            picked[: n * BLOCK, c * 128 : (c + 1) * 128].astype(bf16).reshape(n, BLOCK, 128)
        )
    spilled = jnp.concatenate(
        [picked[n * BLOCK :, c * 128 : (c + 1) * 128] for c in range(chunks)], axis=0
    ).astype(bf16)
    rows_out[:, main:, :] = dot(turn, spilled).astype(bf16).reshape(n, chunks, 128)

    pl.semaphore_wait(barrier, n)
    row_copies = {}
    for k in range(1, n):
        row_copies[k] = push(rows_out.at[k], rows_in.at[k], rows_sem, k, {"adapter": me ^ k})

    loads[4].wait()
    base = dot(hidden[...], value[...])
    first, second = base[:, :half], base[:, half:]
    base_own[...] = jnp.where(core == 0, first, second)
    base_out[...] = jnp.where(core == 0, second, first)
    base_copy = push(base_out, base_in, base_sem, 0, {"tensor": 1 - core})

    rows_in[0] = rows_out[0]
    delta_out[...] = jnp.zeros_like(delta_out)
    low_slot = jnp.where(place < BLOCK, place, 2 * BLOCK) + block_of * SLOTS
    high_slot = jnp.where(place < BLOCK, BLOCK + place, 2 * BLOCK + 1) + block_of * SLOTS
    slot_ids = lax.broadcasted_iota(jnp.int32, (128, rows), 0)
    backs = []
    for group in groups:
        slots = jnp.where(slot_ids < each * SLOTS, slot_ids + group[0] * SLOTS, -1)
        backs.append(
            [
                jnp.transpose((slots == slot).astype(f32))[:, : each * SLOTS].astype(bf16)
                for slot in (low_slot, high_slot)
            ]
        )
    gather_row = lax.broadcasted_iota(jnp.int32, (8 * chunks, each * chunks), 0)
    gather_column = lax.broadcasted_iota(jnp.int32, (8 * chunks, each * chunks), 1)
    turn_back = (gather_row % 8 * chunks + gather_row // 8 == gather_column).astype(bf16)
    loads[2].wait()
    loads[3].wait()
    base_copy.wait_recv()
    base_own[...] = base_own[...] + base_in[...]

    part_copies = []
    delta_copies = {}

    def shrink(g):
        group = groups[g]
        blocks = pl.ds(group[0], each)
        for k in group:
            if k > 0:
                row_copies[k].wait_recv()
        turned = dot(turn_back, rows_in[blocks, main:, :].reshape(each * chunks, 128))
        taken = [
            jnp.concatenate(
                [
                    rows_in[blocks, c * BLOCK : (c + 1) * BLOCK, :].reshape(count, 128),
                    turned[c * 8 : (c + 1) * 8].astype(bf16),
                ],
                axis=0,
            )
            for c in range(chunks)
        ]
        part = lax.dot_general(
            jnp.concatenate(taken, axis=1), down[...], (((1,), (1,)), ((), ())),
            preferred_element_type=f32,
        )
        part_out[g] = jnp.concatenate([part, jnp.zeros((count + 8, 128 - rank), f32)], axis=1)
        part_copies.append(
            push(part_out.at[g], part_in.at[g], part_sem, g, {"tensor": 1 - core})
        )

    def widen(g):
        part_copies[g].wait_recv()
        reduced = (part_out[g] + part_in[g])[:, :rank]
        stacked = jnp.concatenate([x.astype(f32) for x in three_parts(reduced)], axis=0)
        wide = dot(stacked.astype(bf16), up[...])
        size = count + 8
        wide = wide[:size] + wide[size : 2 * size] + wide[2 * size :]
        for i, k in enumerate(groups[g]):
            target = delta_in if k == 0 else delta_out
            if k == 0:
                delta_in[0] = jnp.zeros((SLOTS, 128), f32)
            target[k, :BLOCK] = wide[i * BLOCK : (i + 1) * BLOCK, :128]
            target[k, BLOCK : 2 * BLOCK] = wide[i * BLOCK : (i + 1) * BLOCK, 128:]
            target[k, 2 * BLOCK : 2 * BLOCK + 1] = wide[count + i : count + i + 1, :128]
            target[k, 2 * BLOCK + 1 : 2 * BLOCK + 2] = wide[count + i : count + i + 1, 128:]
            if k > 0:
                delta_copies[k] = push(
                    delta_out.at[k], delta_in.at[k], delta_sem, k, {"adapter": me ^ k}
                )

    for g in range(len(groups)):
        shrink(g)
        if g > 0:
            widen(g - 1)
    widen(len(groups) - 1)

    total = base_own[...]
    for group, back in zip(groups, backs):
        for k in group:
            if k > 0:
                delta_copies[k].wait_recv()
        parts = three_parts(
            delta_in[group[0] : group[0] + each].reshape(each * SLOTS, 128)
        )
        total = total + jnp.concatenate(
            [sum(dot(side, x) for x in parts) for side in back], axis=1
        )
    out_ref[...] = total.astype(out_ref.dtype)

    for copy in sent:
        copy.wait_send()


GROUPS = ((0,), (1,), (2,), (3,), (4,), (5,), (6,), (7,))
SLOTS = 2 * BLOCK + 8


def fused_body(
    hidden_state_rows, value_weight, adapter_down_weight, adapter_up_weight, request_adapter_index
):
    n = lax.axis_size("adapter")
    rows, depth = hidden_state_rows.shape
    width = value_weight.shape[1]
    half = width // 2
    rank = adapter_down_weight.shape[2]
    chunks = depth // 128
    each = len(GROUPS[0])
    dma = pltpu.SemaphoreType.DMA
    return pl.pallas_call(
        functools.partial(adapter_kernel, n, GROUPS),
        out_shape=jax.ShapeDtypeStruct((rows, half), bf16),
        in_specs=[pl.BlockSpec(memory_space=pl.ANY)] * 5,
        out_specs=pl.BlockSpec(memory_space=pltpu.VMEM),
        scratch_shapes=[
            pltpu.VMEM((1, rows), jnp.int32),
            pltpu.VMEM((rows, depth), bf16),
            pltpu.VMEM((depth, width), bf16),
            pltpu.VMEM((rank, depth), bf16),
            pltpu.VMEM((rank, half), bf16),
            pltpu.VMEM((n, chunks * (BLOCK + 1), 128), bf16),
            pltpu.VMEM((n, chunks * (BLOCK + 1), 128), bf16),
            pltpu.VMEM((n // each, each * BLOCK + 8, 128), f32),
            pltpu.VMEM((n // each, each * BLOCK + 8, 128), f32),
            pltpu.VMEM((n, SLOTS, 128), f32),
            pltpu.VMEM((n, SLOTS, 128), f32),
            pltpu.VMEM((rows, half), f32),
            pltpu.VMEM((rows, half), f32),
            pltpu.VMEM((rows, half), f32),
            dma((5,)),
            dma((2, n)),
            dma((2, n // each)),
            dma((2, n)),
            dma((2, 1)),
        ],
        compiler_params=pltpu.CompilerParams(
            collective_id=0, has_side_effects=True, vmem_limit_bytes=60 * 1024 * 1024
        ),
    )(
        request_adapter_index.reshape(1, rows),
        hidden_state_rows,
        value_weight,
        jnp.swapaxes(adapter_down_weight.reshape(depth, rank), 0, 1),
        adapter_up_weight.reshape(rank, half),
    )


def adapter_delta_rows(incoming_rows, down_matrix, up_matrix):
    flat_rows = incoming_rows.reshape(-1, incoming_rows.shape[-1])
    reduced_rows = jnp.dot(flat_rows, down_matrix, preferred_element_type=jnp.float32)
    reduced_rows = lax.psum(reduced_rows, "tensor")
    widened_rows = jnp.dot(
        reduced_rows, up_matrix, precision=highest_precision, preferred_element_type=jnp.float32
    )
    widened_rows = widened_rows.reshape(
        incoming_rows.shape[0], incoming_rows.shape[1], up_matrix.shape[1]
    )
    return lax.all_to_all(widened_rows, "adapter", split_axis=0, concat_axis=0, tiled=True)


def general_body(
    hidden_state_rows, value_weight, adapter_down_weight, adapter_up_weight, request_adapter_index
):
    holders = lax.axis_size("adapter")
    rows_here = hidden_state_rows.shape[0]
    slots_per_pair = 2 + (rows_here - 1) // holders
    holder_ids = lax.broadcasted_iota(jnp.int32, (rows_here, holders), 1)
    onehot = (request_adapter_index[:, None] == holder_ids).astype(jnp.int32)
    pair_ranks = jnp.sum(onehot * (jnp.cumsum(onehot, axis=0) - 1), axis=1)
    slot_index = request_adapter_index * slots_per_pair + pair_ranks
    down_matrix = adapter_down_weight[0]
    up_matrix = adapter_up_weight[0].astype(jnp.float32)
    slot_ids = lax.broadcasted_iota(jnp.int32, (holders * slots_per_pair, rows_here), 0)
    placing = (slot_ids == slot_index[None, :]).astype(hidden_state_rows.dtype)
    send_rows = jnp.dot(placing, hidden_state_rows, preferred_element_type=jnp.float32).astype(
        hidden_state_rows.dtype
    )
    send_rows = send_rows.reshape(holders, slots_per_pair, hidden_state_rows.shape[1])
    value_result = adapter_delta_rows(
        lax.all_to_all(send_rows, "adapter", split_axis=0, concat_axis=0, tiled=True),
        down_matrix,
        up_matrix,
    )
    delta_rows = jnp.take(value_result.reshape(holders * slots_per_pair, -1), slot_index, axis=0)
    base_terms = jnp.dot(hidden_state_rows, value_weight, preferred_element_type=jnp.float32)
    own_columns = lax.psum_scatter(base_terms, "tensor", scatter_dimension=1, tiled=True)
    summed = own_columns + delta_rows
    return summed.astype(jnp.bfloat16)


def body(*arrays):
    n = lax.axis_size("adapter")
    if n == 8 and arrays[0].shape[0] == n * BLOCK:
        return fused_body(*arrays)
    return general_body(*arrays)


def solution(mesh):
    return jax.shard_map(
        body,
        mesh=mesh,
        in_specs=(
            P(("groups", "adapter"), "tensor"),
            P("tensor", None),
            P(("groups", "adapter"), "tensor", None),
            P(("groups", "adapter"), None, "tensor"),
            P(("groups", "adapter")),
        ),
        out_specs=P(("groups", "adapter"), "tensor"),
        check_vma=False,
    )
```

time: 39.3 us -> 38.9 us (0.990)
  Pallas kernels: 37.6 us -> 37.2 us
    pallas_call x1, Pallas kernels: 37.6 us -> 37.2 us  [fused_body(): pl.pallas_call(functools.partial(adapter_kernel, n, GROUPS), out_shape=ja...]
where the time goes in v3:
time: 38.9 us; the launch traced here: 38.7 us
  Pallas kernels  37.2 us (96%)
  local copies, waits for them, and re-layouts  1.47 us (4%)
    pallas_call x1, Pallas kernels, fused_body(): pl.pallas_call(functools.partial(adapter_kernel, n, GROUPS), out_shape=ja...  37.2 us
    unnamed x1, local copies, waits for them, and re-layouts  1.47 us

profile of v3, /device:TPU:9, one launch (start us, length us, event | category | flops | bytes accessed | tf_op | source)
XLA Modules:
  0.0 38.7 jit_solution(16706266448409651703)
XLA Ops:
  0.0 37.2 %shard_map.55 = bf16[128,256]{1,0:T(8,128)(2,1)} custom-call(s32[1,128]{1,0:T(1,128)} %bitcast.7, bf16[128,4096]{1,0:T(8,128)(2,1)} %hidden_hbm.1, bf16[4096,512]{1,0:T(8,128)(2,1)} %value_hbm.1, bf16[64,4096]{1,0:T(8,128)(2,1)} %bitcast.5, bf16[64,256]{1,0:T(8,128)(2,1)} %bitcast.6), custom_call_target="tpu_custom_call" | custom-call | tf_op jit(solution)/shard_map/pallas_call | solution.py:225
  37.2 1.5 %copy.7 = bf16[128,256]{1,0:T(8,128)(2,1)} copy(bf16[128,256]{1,0:T(8,128)(2,1)} %shard_map.55) | data formatting | bytes 131072

commit v4 on v3

--- a/solution.py
+++ b/solution.py
@@ -53,6 +53,7 @@
     ]
     loads[0].start()
     loads[1].start()
+    delta_in[:, 2 * BLOCK :] = jnp.zeros((n, SLOTS - 2 * BLOCK, 128), f32)
 
     barrier = pltpu.get_barrier_semaphore()
     for k in range(1, n):
@@ -181,7 +182,7 @@
             target[k, 2 * BLOCK + 1 : 2 * BLOCK + 2] = wide[count + i : count + i + 1, 128:]
             if k > 0:
                 delta_copies[k] = push(
-                    delta_out.at[k], delta_in.at[k], delta_sem, k, {"adapter": me ^ k}
+                    delta_out.at[k, :FILLED], delta_in.at[k, :FILLED], delta_sem, k, {"adapter": me ^ k}
                 )
 
     for g in range(len(groups)):
@@ -209,6 +210,7 @@
 
 GROUPS = ((0,), (1,), (2,), (3,), (4,), (5,), (6,), (7,))
 SLOTS = 2 * BLOCK + 8
+FILLED = 2 * BLOCK + 2
 
 
 def fused_body(

time: 38.9 us -> 38.4 us (0.987)
  Pallas kernels: 37.2 us -> 36.8 us
    pallas_call x1, Pallas kernels: 37.2 us -> 36.8 us  [fused_body(): pl.pallas_call(functools.partial(adapter_kernel, n, GROUPS), out_shape=ja...]
where the time goes in v4:
time: 38.4 us; the launch traced here: 38.3 us
  Pallas kernels  36.8 us (96%)
  local copies, waits for them, and re-layouts  1.47 us (4%)
    pallas_call x1, Pallas kernels, fused_body(): pl.pallas_call(functools.partial(adapter_kernel, n, GROUPS), out_shape=ja...  36.8 us
    unnamed x1, local copies, waits for them, and re-layouts  1.47 us

profile of v4, /device:TPU:9, one launch (start us, length us, event | category | flops | bytes accessed | tf_op | source)
XLA Modules:
  0.0 38.3 jit_solution(93126001598405364)
XLA Ops:
  0.0 36.8 %shard_map.55 = bf16[128,256]{1,0:T(8,128)(2,1)} custom-call(s32[1,128]{1,0:T(1,128)} %bitcast.7, bf16[128,4096]{1,0:T(8,128)(2,1)} %hidden_hbm.1, bf16[4096,512]{1,0:T(8,128)(2,1)} %value_hbm.1, bf16[64,4096]{1,0:T(8,128)(2,1)} %bitcast.5, bf16[64,256]{1,0:T(8,128)(2,1)} %bitcast.6), custom_call_target="tpu_custom_call" | custom-call | tf_op jit(solution)/shard_map/pallas_call | solution.py:227
  36.8 1.5 %copy.7 = bf16[128,256]{1,0:T(8,128)(2,1)} copy(bf16[128,256]{1,0:T(8,128)(2,1)} %shard_map.55) | data formatting | bytes 131072

commit v5 on v4

--- a/solution.py
+++ b/solution.py
@@ -92,20 +92,29 @@
     loads[1].wait()
     for load in loads[2:]:
         load.start()
-    picked = dot(pick, hidden[...])
-    for c in range(chunks):
-        rows_out[:, c * BLOCK : (c + 1) * BLOCK, :] = (
-            picked[: n * BLOCK, c * 128 : (c + 1) * 128].astype(bf16).reshape(n, BLOCK, 128)
-        )
-    spilled = jnp.concatenate(
-        [picked[n * BLOCK :, c * 128 : (c + 1) * 128] for c in range(chunks)], axis=0
-    ).astype(bf16)
-    rows_out[:, main:, :] = dot(turn, spilled).astype(bf16).reshape(n, chunks, 128)
-
-    pl.semaphore_wait(barrier, n)
     row_copies = {}
-    for k in range(1, n):
-        row_copies[k] = push(rows_out.at[k], rows_in.at[k], rows_sem, k, {"adapter": me ^ k})
+    spilled = []
+    for part in range(2):
+        first, last = part * chunks // 2, (part + 1) * chunks // 2
+        picked = dot(pick, hidden[:, first * 128 : last * 128])
+        for c in range(first, last):
+            piece = picked[:, (c - first) * 128 : (c - first + 1) * 128]
+            rows_out[:, c * BLOCK : (c + 1) * BLOCK, :] = (
+                piece[: n * BLOCK].astype(bf16).reshape(n, BLOCK, 128)
+            )
+            spilled.append(piece[n * BLOCK :])
+        if part == 0:
+            pl.semaphore_wait(barrier, n)
+            region = pl.ds(0, main // 2)
+        else:
+            turned = dot(turn, jnp.concatenate(spilled, axis=0).astype(bf16))
+            rows_out[:, main:, :] = turned.astype(bf16).reshape(n, chunks, 128)
+            region = pl.ds(main // 2, main // 2 + chunks)
+        for k in range(1, n):
+            row_copies[part * n + k] = push(
+                rows_out.at[k, region], rows_in.at[k, region], rows_sem, part * n + k,
+                {"adapter": me ^ k},
+            )
 
     loads[4].wait()
     base = dot(hidden[...], value[...])
@@ -145,6 +154,7 @@
         for k in group:
             if k > 0:
                 row_copies[k].wait_recv()
+                row_copies[n + k].wait_recv()
         turned = dot(turn_back, rows_in[blocks, main:, :].reshape(each * chunks, 128))
         taken = [
             jnp.concatenate(
@@ -245,7 +255,7 @@
             pltpu.VMEM((rows, half), f32),
             pltpu.VMEM((rows, half), f32),
             dma((5,)),
-            dma((2, n)),
+            dma((2, 2 * n)),
             dma((2, n // each)),
             dma((2, n)),
             dma((2, 1)),

time: 38.4 us -> 40 us (1.042)
  the two profiles are of different devices: /device:TPU:9 before, /device:TPU:0 now
where the time goes in v5:
time: 40 us; the launch traced here: 39.9 us
  Pallas kernels  38.4 us (96%)
  local copies, waits for them, and re-layouts  1.47 us (4%)
    pallas_call x1, Pallas kernels, fused_body(): pl.pallas_call(functools.partial(adapter_kernel, n, GROUPS), out_shape=ja...  38.4 us
    unnamed x1, local copies, waits for them, and re-layouts  1.47 us

profile of v5, /device:TPU:0, one launch (start us, length us, event | category | flops | bytes accessed | tf_op | source)
XLA Modules:
  0.0 39.9 jit_solution(4066742778917066687)
XLA Ops:
  0.0 38.4 %shard_map.55 = bf16[128,256]{1,0:T(8,128)(2,1)} custom-call(s32[1,128]{1,0:T(1,128)} %bitcast.7, bf16[128,4096]{1,0:T(8,128)(2,1)} %hidden_hbm.1, bf16[4096,512]{1,0:T(8,128)(2,1)} %value_hbm.1, bf16[64,4096]{1,0:T(8,128)(2,1)} %bitcast.5, bf16[64,256]{1,0:T(8,128)(2,1)} %bitcast.6), custom_call_target="tpu_custom_call" | custom-call | tf_op jit(solution)/shard_map/pallas_call | solution.py:237
  38.4 1.5 %copy.7 = bf16[128,256]{1,0:T(8,128)(2,1)} copy(bf16[128,256]{1,0:T(8,128)(2,1)} %shard_map.55) | data formatting | bytes 131072
